TPU v7x, 32 devices: a whole 2x2x4 slice. The times are simulated.
32 devices in a mesh: groups: 2 (over x), tensor: 8 (over z, y), seq: 2 (over core).
Axes of the slice: x: 2, y: 2, z: 4, core: 2. Of those that a mesh axis runs over, the one named last changes fastest.
Arguments:
- queries: bfloat16 [64, 64, 128], P('groups'), parts along dimension 0
- keys: bfloat16 [32768, 64, 128], P(('tensor', 'seq'), 'groups'), parts along dimension 1
- values: bfloat16 [32768, 64, 128], P(('tensor', 'seq'), 'groups'), parts along dimension 1, may hold values from -6 to 6
- lengths: int32 [64], P('groups'), parts along dimension 0, may hold values from 2 to 4096, as said below
- out_weight: bfloat16 [8192, 8192], P(('tensor', 'seq')), may hold values from -0.75 to 0.75
Outputs:
- mixed: bfloat16 [64, 8192], P('groups', ('tensor', 'seq')), parts along dimension 0
There are 2 independent parts, one for each index of `groups`. A program takes and returns all parts, laid end to end along the dimension named above; an argument that names none is the same for every part. Nothing has to cross between parts.
Inputs may be any that keep to these rules, and one draw needn't show every extreme that they name: `lengths`: every length is at least 2, and in each part one sequence has exactly 4096 live slots.
All inputs are finite; a program needn't handle non-finite values.
Results may differ from a plain program's by a relative error of at most 0.005.
Values sent between devices are 32-bit elements; how exact they have to be, the bound alone decides.
A program may use at most 128 MiB of HBM per device.

v0:
```python
import math

import jax
import jax.numpy as jnp
from jax import lax
from jax.sharding import PartitionSpec as P

HQ = 64
KVH = 8
CACHE = 4096


masked_fill = -1e30


def swapped(block, axis, apart):
    count = lax.axis_size(axis)
    route = []
    for low in range(count):
        high = low | 1 << apart
        if high != low and high < count:
            route += [(low, high), (high, low)]
    return lax.ppermute(block, axis, route)


def combine(first, second):
    high_a, total_a, accum_a = first
    high_b, total_b, accum_b = second
    highest = jnp.maximum(high_a, high_b)
    scale_a = jnp.exp(high_a - highest)
    scale_b = jnp.exp(high_b - highest)
    return (
        highest,
        total_a * scale_a + total_b * scale_b,
        accum_a * scale_a[..., None] + accum_b * scale_b[..., None],
    )


def halves(stats, own_bit):
    count = stats[0].shape[1] // 2
    lower = jax.tree.map(lambda member: member[:, :count], stats)
    upper = jax.tree.map(lambda member: member[:, count:], stats)
    keep = jax.tree.map(lambda first, second: jnp.where(own_bit == 1, second, first), lower, upper)
    send = jax.tree.map(lambda first, second: jnp.where(own_bit == 1, first, second), lower, upper)
    return (keep, send)


def body(queries, keys, values, lengths, out_weight):
    n_tensor = lax.axis_size("tensor")
    n_seq = lax.axis_size("seq")
    replicas = n_tensor // KVH
    tensor_index = lax.axis_index("tensor")
    seq_index = lax.axis_index("seq")
    flat_index = tensor_index * n_seq + seq_index
    span = keys.shape[0]
    batch = keys.shape[1]
    head_size = keys.shape[2]
    per_group = HQ // KVH
    start = flat_index * span
    kv_head = start // CACHE
    first_slot = start % CACHE
    group_queries = lax.dynamic_slice_in_dim(queries, kv_head * per_group, per_group, 1)
    scores = jnp.einsum(
        "bgd,pbd->bgp", group_queries, keys, preferred_element_type=jnp.float32
    ) / math.sqrt(head_size)
    positions = first_slot + jnp.arange(span, dtype=jnp.int32)
    live = (positions[None, :] < lengths[:, None])[:, None, :]
    scores = jnp.where(live, scores, masked_fill)
    highest = jnp.max(scores, axis=2)
    weights = jnp.where(live, jnp.exp(scores - highest[..., None]), 0.0)
    totals = jnp.sum(weights, axis=2)
    accum = jnp.einsum(
        "bgp,pbd->bgd", weights, values.astype(jnp.float32), precision=lax.Precision.HIGHEST
    )
    stats = (highest, totals, accum)
    tensor_levels = replicas.bit_length() - 1
    seq_levels = n_seq.bit_length() - 1
    for level in reversed(range(tensor_levels)):
        keep, send = halves(stats, tensor_index >> level & 1)
        stats = combine(keep, swapped(send, "tensor", level))
    for level in reversed(range(seq_levels)):
        keep, send = halves(stats, seq_index >> level & 1)
        stats = combine(keep, swapped(send, "seq", level))
    highest, totals, accum = stats
    attended = (accum / totals[..., None]).astype(jnp.bfloat16).reshape(batch, -1)
    mixed_rows = lax.psum_scatter(
        lax.dot_general(
            out_weight, attended, (((0,), (1,)), ((), ())), preferred_element_type=jnp.float32
        ),
        ("tensor", "seq"),
        scatter_dimension=0,
        tiled=True,
    )
    return mixed_rows.T.astype(jnp.bfloat16)


def solution(mesh):
    return jax.shard_map(
        body,
        mesh=mesh,
        in_specs=(
            P("groups", None, None),
            P(("tensor", "seq"), "groups", None),
            P(("tensor", "seq"), "groups", None),
            P("groups"),
            P(("tensor", "seq"), None),
        ),
        out_specs=P("groups", ("tensor", "seq")),
        check_vma=False,
    )
```

profile of v0, /device:TPU:0, one launch (start us, length us, event | category | flops | bytes accessed | tf_op | source)
XLA Modules:
  0.0 111.0 jit_solution(10238446696510164654)
XLA Ops:
  6.5 0.0 copy-start
  6.5 0.0 reduce-scatter.2.cloned.1.call-start
  6.5 0.8 broadcast_compare_fusion
  7.4 0.2 copy-done
  7.6 15.2 %fusion.24 = (f32[32,8]{1,0:T(8,128)S(1)}, f32[32,8,2048]{2,1,0:T(8,128)S(1)}) fusion(bf16[2048,32,128]{2,1,0:T(8,128)(2,1)} %param.6, bf16[32,64,128]{2,1,0:T(8,128)(2,1)S(1)} %copy-done, s32[]{:T(128)S(6)} %select_n.56, pred[32,2048]{1,0:T(8,128)(4,1)S(1)} %broadcast_compare_fusion), kind=kOutput, calls=%fused_computation.31 | convolution fusion | flops 135790336 | bytes 19006468 | tf_op jit(solution)/shard_map/bgd,pbd->bgp/dot_general | solution.py:63
  22.8 0.1 slice_select_fusion.2
  22.9 0.5 collective-permute-start
  23.3 0.6 fusion.10
  24.0 0.0 slice-start
  24.0 0.1 slice_select_fusion.1
  24.1 0.1 collective-permute-start.2
  24.1 14.1 %fusion = f32[32,8,128]{2,1,0:T(8,128)S(1)} fusion(bf16[2048,32,128]{2,1,0:T(8,128)(2,1)} %param.7, f32[32,8,2048]{2,1,0:T(8,128)S(1)} %get-tuple-element.9, f32[32,8]{1,0:T(8,128)S(1)} %get-tuple-element.8, pred[32,2048]{1,0:T(8,128)(4,1)S(1)} %broadcast_compare_fusion), kind=kOutput, calls=%fused_computation | convolution fusion | flops 806354944 | bytes 19072000 | tf_op jit(solution)/shard_map/bgp,pbd->bgd/dot_general | solution.py:72
  38.3 0.6 collective-permute-start.1
  38.9 0.0 collective-permute-done
  38.9 0.0 collective-permute-done.2
  38.9 0.1 multiply_add_fusion
  39.0 0.8 collective-permute-done.1
  39.8 0.2 fusion.15
  40.0 0.0 slice-done
  40.0 0.0 slice-done.1
  40.0 2.5 %convolution_bitcast_fusion = f32[8192,32]{0,1:T(8,128)} fusion(bf16[512,8192]{1,0:T(8,128)(2,1)S(1)} %bitcast.10, bf16[4,8,4,128]{3,2,1,0:T(4,128)(2,1)S(1)} %bitcast.11), kind=kOutput, calls=%fused_computation.4 | convolution fusion | flops 268435456 | bytes 9469952 | tf_op jit(solution)/shard_map/dot_general | solution.py:87
  42.5 0.0 reduce-scatter.2.cloned.1.call-update
  42.5 60.2 %reduce-scatter.2.cloned.1.call-done = f32[512,32]{0,1:T(8,128)} async-done(((f32[8192,32]{0,1:T(8,128)}), f32[512,32]{0,1:T(8,128)}) %reduce-scatter.2.cloned.1.call-update) | async-done | bytes 65552 | tf_op jit(solution)/shard_map/reduce_scatter | solution.py:86
  102.7 1.5 %convert_bitcast_fusion = bf16[32,512]{1,0:T(8,128)(2,1)} fusion(f32[512,32]{0,1:T(8,128)} %reduce-scatter.2.cloned.1.call-done), kind=kLoop, calls=%fused_computation.19 | loop fusion | flops 16384 | bytes 98304 | tf_op jit(solution)/shard_map/convert_element_type | solution.py:94
  (4 shorter events, 0.0 us)
Async XLA Ops:
  6.5 1.1 copy-start
  6.5 96.2 %reduce-scatter.2.cloned.1.call-start = ((), (), s32[]{:S(2)}) async-start(), calls=%async_computation.1 | async-start | bytes 1114112 | tf_op jit(solution)/shard_map/reduce_scatter | solution.py:86
  22.9 16.0 %collective-permute-start = (f32[32,4]{1,0:T(8,128)S(1)}, f32[32,4]{1,0:T(8,128)S(1)}, u32[]{:S(2)}, u32[]{:S(2)}) collective-permute-start(f32[32,4]{1,0:T(8,128)S(1)} %slice_select_fusion.2), channel_id=1, source_target_pairs={{0,1},{1,0},{2,3},{3,2},{4,5},{5,4},{6,7},{7,6},{8,9},{9,8},{10,11... | collective-permute-start | bytes 1544 | tf_op jit(solution)/shard_map/ppermute | solution.py:23
  24.0 16.0 %slice-start = ((s8[8388608]{0:T(1024)(128)(4,1)}), s8[4194304]{0:T(1024)(128)(4,1)S(1)}, s32[]{:S(2)}) async-start(s8[8388608]{0:T(1024)(128)(4,1)} %bitcast.9), calls=%async_computation.2 | async-start | bytes 8388608
  24.1 15.9 %slice-start.1 = ((s8[8388608]{0:T(1024)(128)(4,1)}), s8[4194304]{0:T(1024)(128)(4,1)S(1)}, s32[]{:S(2)}) async-start(s8[8388608]{0:T(1024)(128)(4,1)} %bitcast.9), calls=%async_computation.3 | async-start | bytes 8388608
  24.1 14.8 %collective-permute-start.2 = (f32[32,4]{1,0:T(8,128)S(1)}, f32[32,4]{1,0:T(8,128)S(1)}, u32[]{:S(2)}, u32[]{:S(2)}) collective-permute-start(f32[32,4]{1,0:T(8,128)S(1)} %slice_select_fusion.1), channel_id=1, source_target_pairs={{0,1},{1,0},{2,3},{3,2},{4,5},{5,4},{6,7},{7,6},{8,9},{9,8},{10,11... | collective-permute-start | bytes 1544 | tf_op jit(solution)/shard_map/ppermute | solution.py:23
  38.3 1.5 %collective-permute-start.1 = (f32[32,4,128]{2,1,0:T(4,128)S(1)}, f32[32,4,128]{2,1,0:T(4,128)S(1)}, u32[]{:S(2)}, u32[]{:S(2)}) collective-permute-start(f32[32,4,128]{2,1,0:T(4,128)S(1)} %slice_select_fusion), channel_id=1, source_target_pairs={{0,1},{1,0},{2,3},{3,2},{4,5},{5,4},{6,7},{7,6},{8,9},{9,8},{10,11... | collective-permute-start | bytes 196616 | tf_op jit(solution)/shard_map/ppermute | solution.py:23
Sparse Core Ops, SparseCore 0:
  42.6 60.0 reduce-scatter.1
where the time goes:
time: 111 us
  waiting for transfers between devices  61 us (55%)
  matrix products  31.8 us (29%)
  between operations  13.5 us (12%)
  other arithmetic  3.33 us (3%)
  starting transfers between devices  1.15 us (1%)
    reduce_scatter x1, waiting for transfers between devices, body(): lax.psum_scatter(lax.dot_general(out_weight, attended, (((0,), (1,)), (()...  60.2 us
    dot_general x1, matrix products, body(): jnp.einsum('bgd,pbd->bgp', group_queries, keys, preferred_element_type=jn...  15.2 us
    dot_general x1, matrix products, body(): jnp.einsum('bgp,pbd->bgd', weights, values.astype(jnp.float32), precision...  14.1 us
    dot_general x1, matrix products, body(): lax.dot_general(out_weight, attended, (((0,), (1,)), ((), ())), preferred...  2.52 us
  transfers between devices with their start and end apart: 4, of which 2 were waited for; matrix products, arithmetic and copies ran while one was open for 13% of the time, Pallas kernels for 0%

commit v1 on v0

v1 whole, which is shorter than its diff:
```python
import functools
import math

import jax
import jax.numpy as jnp
from jax import lax
from jax.experimental import pallas as pl
from jax.experimental.pallas import tpu as pltpu
from jax.sharding import PartitionSpec as P

HQ = 64
KVH = 8
CACHE = 4096

MESH = pl.DeviceIdType.MESH
masked_fill = -1e30
ROWS = 16
STEP = 64


def kernel(
    n_tensor, n_seq, lengths, queries, keys, values, weight, out,
    kbuf, vbuf, wbuf, qbuf, qflat, qdiag, scores, acc, stats, got, flat_att,
    part, from_core, pair, from_near, line, from_far,
    k_sem, v_sem, w_sem, q_sem, stat_sems, core_sems, near_sems, far_sems,
):
    n_flat = n_tensor * n_seq
    span, batch, head_size = keys.shape
    per_group = HQ // KVH
    n_split = CACHE // span
    groups = batch // ROWS
    lanes = ROWS * per_group
    wide = groups * lanes
    depth = groups * head_size
    heads_own = HQ // n_flat
    n_chunks = span // STEP
    cols = out.shape[1]
    n_far = n_tensor // 2
    wide_cols = 2 * n_seq * cols

    group = lax.axis_index("groups")
    tensor = lax.axis_index("tensor")
    core = lax.axis_index("seq")
    flat = tensor * n_seq + core
    kv_head = flat // n_split
    place = flat % n_split
    far, near = tensor // 2, tensor % 2
    other_core = 1 - core

    offsets = sorted(range(n_far), key=lambda off: (-min(off, n_far - off), off))

    def member(index):
        return (group, index // n_seq, index % n_seq)

    stat_peers = [member(kv_head * n_split + (place + k) % n_split) for k in range(1, n_split)]
    core_peer = (group, tensor, other_core)
    near_peer = (group, far * 2 + 1 - near, core)
    far_peers = [(group, (far + off) % n_far * 2 + near, core) for off in offsets]

    barrier = pltpu.get_barrier_semaphore()
    greeted = stat_peers + [core_peer, near_peer] + [
        peer for off, peer in zip(offsets, far_peers) if off
    ]
    for peer in greeted:
        pl.semaphore_signal(barrier, inc=1, device_id=peer, device_id_type=MESH)

    q_rows = ROWS if per_group < ROWS else per_group
    q_start = pl.multiple_of(kv_head * per_group // q_rows * q_rows, q_rows)
    q_copy = pltpu.make_async_copy(queries.at[:, pl.ds(q_start, q_rows), :], qbuf, q_sem)
    q_copy.start()

    def k_copy(c):
        piece = pl.ds(c * STEP, STEP)
        return pltpu.make_async_copy(keys.at[piece], kbuf.at[piece], k_sem.at[c])

    def v_copy(c):
        piece = pl.ds(c * STEP, STEP)
        return pltpu.make_async_copy(values.at[piece], vbuf.at[piece], v_sem.at[c])

    def w_copy(k):
        start = pl.multiple_of((far + offsets[k]) % n_far * wide_cols, wide_cols)
        return pltpu.make_async_copy(weight.at[:, pl.ds(start, wide_cols)], wbuf.at[k], w_sem.at[k])

    @pl.loop(0, n_chunks)
    def _(c):
        k_copy(c).start()

    @pl.loop(0, n_chunks)
    def _(c):
        v_copy(c).start()

    for k in range(n_far):
        w_copy(k).start()

    lane = lax.broadcasted_iota(jnp.int32, (8, wide), 1)
    sub = lax.broadcasted_iota(jnp.int32, (8, wide), 0)
    home = lane % 8
    low = lane % ROWS < 8
    turn = (sub - home + 8) % 8
    at_home = sub == home
    sequence = lane // lanes * ROWS + lane % ROWS
    live_slots = jnp.zeros((8, wide), jnp.int32)
    for b in range(batch):
        live_slots = jnp.where(sequence == b, lengths[b], live_slots)
    first_slot = place * span
    room = live_slots - first_slot - turn

    q_copy.wait()
    q = qbuf[...].astype(jnp.float32)
    if q_rows > per_group:
        q = jnp.where(kv_head % 2 == 0, q[:, :per_group], q[:, per_group:])
    qflat[...] = q
    zero = jnp.zeros((head_size, lanes), jnp.bfloat16)
    for g in range(groups):
        block = jnp.concatenate(
            [qflat[g * ROWS:(g + 1) * ROWS, j, :] for j in range(per_group)], axis=0
        )
        for h in range(groups):
            qdiag[g * head_size:(g + 1) * head_size, h * lanes:(h + 1) * lanes] = (
                block.T.astype(jnp.bfloat16) if g == h else zero
            )

    def side_by_side(buf, c):
        piece = buf[pl.ds(c * STEP, STEP)]
        return jnp.concatenate(
            [
                piece[:, g * ROWS:(g + 1) * ROWS].reshape(STEP * ROWS, head_size)
                for g in range(groups)
            ],
            axis=1,
        )

    blocks = STEP // 8

    def base_of(c):
        return c * STEP + 8 * lax.broadcasted_iota(jnp.int32, (blocks, 8, wide), 0)

    def score_step(c, highest):
        k_copy(c).wait()
        product = jnp.dot(side_by_side(kbuf, c), qdiag[...], preferred_element_type=jnp.float32)
        product = product.reshape(blocks, 8, 2, 8, wide)
        merged = jnp.where(low, product[:, :, 0], product[:, :, 1])
        dense = merged[:, 0]
        for i in range(1, 8):
            dense = jnp.where(turn == i, pltpu.roll(merged[:, i], i, 1), dense)
        dense = jnp.where(base_of(c) < room, dense, masked_fill)
        scores[pl.ds(c * blocks, blocks)] = dense
        return jnp.maximum(highest, jnp.max(dense, axis=0))

    highest = lax.fori_loop(0, n_chunks, score_step, jnp.full((8, wide), masked_fill, jnp.float32))
    highest = jnp.broadcast_to(jnp.max(highest, axis=0, keepdims=True), (8, wide))
    scale = 1.0 / math.sqrt(head_size)

    acc[...] = jnp.zeros_like(acc)
    keep_low = at_home & low
    keep_high = at_home & jnp.logical_not(low)

    def value_step(c, totals):
        v_copy(c).wait()
        dense = scores[pl.ds(c * blocks, blocks)]
        share = jnp.where(base_of(c) < room, jnp.exp((dense - highest) * scale), 0.0)
        spread = []
        for i in range(8):
            turned = pltpu.roll(share, 8 - i, 1) if i else share
            spread.append(
                jnp.concatenate(
                    [jnp.where(keep_low, turned, 0.0), jnp.where(keep_high, turned, 0.0)], axis=1
                ).astype(jnp.bfloat16)
            )
        spread = jnp.stack(spread, axis=1).reshape(STEP * ROWS, wide)
        piece = vbuf[pl.ds(c * STEP, STEP)]
        for g in range(groups):
            acc[g] += lax.dot_general(
                piece[:, g * ROWS:(g + 1) * ROWS].reshape(STEP * ROWS, head_size),
                spread[:, g * lanes:(g + 1) * lanes],
                (((0,), (0,)), ((), ())),
                preferred_element_type=jnp.float32,
            )
        return totals + jnp.sum(share, axis=0)

    totals = lax.fori_loop(0, n_chunks, value_step, jnp.zeros((8, wide), jnp.float32))
    totals = jnp.broadcast_to(jnp.sum(totals, axis=0, keepdims=True), (8, wide))
    for g in range(groups):
        stats[0:head_size, g * lanes:(g + 1) * lanes] = acc[g]
    stats[head_size:head_size + 8] = highest
    stats[head_size + 8:head_size + 16] = totals

    pl.semaphore_wait(barrier, len(greeted))

    sends = []

    def send(source, target, sems, slot, peer):
        copy = pltpu.make_async_remote_copy(
            src_ref=source, dst_ref=target, send_sem=sems.at[0, slot], recv_sem=sems.at[1, slot],
            device_id=peer, device_id_type=MESH,
        )
        copy.start()
        sends.append(copy)
        return copy

    stat_copies = [
        send(stats, got.at[i], stat_sems, i, peer) for i, peer in enumerate(stat_peers)
    ]
    for copy in stat_copies:
        copy.wait_recv()
    tops = [stats[head_size:head_size + 1]] + [
        got[i, head_size:head_size + 1] for i in range(n_split - 1)
    ]
    top = functools.reduce(jnp.maximum, tops)
    total = jnp.zeros((1, wide), jnp.float32)
    summed = jnp.zeros((head_size, wide), jnp.float32)
    for i in range(n_split):
        source = stats if i == 0 else got.at[i - 1]
        factor = jnp.exp((tops[i] - top) * scale)
        total = total + source[head_size + 8:head_size + 9] * factor
        summed = summed + source[0:head_size] * factor
    summed = summed / total
    for g in range(groups):
        flat_att[g] = summed[:, g * lanes:(g + 1) * lanes].T
    start = pl.multiple_of(place * heads_own * ROWS, ROWS)
    attended = jnp.concatenate(
        [
            jnp.concatenate(
                [flat_att[g, pl.ds(start + j * ROWS, ROWS), :] for j in range(heads_own)], axis=1
            )
            for g in range(groups)
        ],
        axis=0,
    ).astype(jnp.bfloat16)

    core_copies, near_copies, far_copies = [], [], []
    for step in range(n_far + 2):
        if step < n_far:
            w_copy(step).wait()
            for n in range(2):
                for s in range(n_seq):
                    at = (n * n_seq + s) * cols
                    part[step, s, n] = jnp.dot(
                        attended, wbuf[step, :, at:at + cols], preferred_element_type=jnp.float32
                    )
            core_copies.append(
                send(part.at[step, other_core], from_core.at[step], core_sems, step, core_peer)
            )
        k = step - 1
        if 0 <= k < n_far:
            core_copies[k].wait_recv()
            pair[k] = part[k, core] + from_core[k]
            near_copies.append(
                send(pair.at[k, 1 - near], from_near.at[k], near_sems, k, near_peer)
            )
        k = step - 2
        if 0 <= k < n_far:
            near_copies[k].wait_recv()
            line[k] = pair[k, near] + from_near[k]
            if offsets[k]:
                far_copies.append(send(line.at[k], from_far.at[k], far_sems, k, far_peers[k]))
    result = line[n_far - 1]
    for k, copy in enumerate(far_copies):
        copy.wait_recv()
        result = result + from_far[k]
    out[...] = result.astype(out.dtype)
    for copy in sends:
        copy.wait_send()


def solution(mesh):
    n_tensor, n_seq = mesh.shape["tensor"], mesh.shape["seq"]

    def body(queries, keys, values, lengths, out_weight):
        span, batch, head_size = keys.shape
        depth, width = out_weight.shape
        per_group = HQ // KVH
        n_flat = n_tensor * n_seq
        cols = width // n_flat
        n_far = n_tensor // 2
        n_split = CACHE // span
        groups = batch // ROWS
        lanes = ROWS * per_group
        wide = groups * lanes
        n_chunks = span // STEP
        q_rows = max(ROWS, per_group)
        f32, bf16 = jnp.float32, jnp.bfloat16
        peers = max(1, n_split - 1)
        return pl.pallas_call(
            functools.partial(kernel, n_tensor, n_seq),
            out_shape=jax.ShapeDtypeStruct((batch, cols), bf16),
            in_specs=[pl.BlockSpec(memory_space=pltpu.SMEM)] + [pl.BlockSpec(memory_space=pl.ANY)] * 4,
            out_specs=pl.BlockSpec(memory_space=pltpu.VMEM),
            scratch_shapes=[
                pltpu.VMEM((span, batch, head_size), bf16),
                pltpu.VMEM((span, batch, head_size), bf16),
                pltpu.VMEM((n_far, depth, 2 * n_seq * cols), bf16),
                pltpu.VMEM((batch, q_rows, head_size), bf16),
                pltpu.VMEM((batch, per_group, head_size), f32),
                pltpu.VMEM((groups * head_size, wide), bf16),
                pltpu.VMEM((span // 8, 8, wide), f32),
                pltpu.VMEM((groups, head_size, lanes), f32),
                pltpu.VMEM((head_size + 16, wide), f32),
                pltpu.VMEM((peers, head_size + 16, wide), f32),
                pltpu.VMEM((groups, lanes, head_size), f32),
                pltpu.VMEM((n_far, n_seq, 2, batch, cols), f32),
                pltpu.VMEM((n_far, 2, batch, cols), f32),
                pltpu.VMEM((n_far, 2, batch, cols), f32),
                pltpu.VMEM((n_far, batch, cols), f32),
                pltpu.VMEM((n_far, batch, cols), f32),
                pltpu.VMEM((n_far, batch, cols), f32),
                pltpu.SemaphoreType.DMA((n_chunks,)),
                pltpu.SemaphoreType.DMA((n_chunks,)),
                pltpu.SemaphoreType.DMA((n_far,)),
                pltpu.SemaphoreType.DMA,
                pltpu.SemaphoreType.DMA((2, peers)),
                pltpu.SemaphoreType.DMA((2, n_far)),
                pltpu.SemaphoreType.DMA((2, n_far)),
                pltpu.SemaphoreType.DMA((2, n_far)),
            ],
            compiler_params=pltpu.CompilerParams(
                collective_id=0, has_side_effects=True, vmem_limit_bytes=60 * 1024 * 1024
            ),
            cost_estimate=pl.CostEstimate(
                flops=4 * span * batch * head_size * per_group + 2 * batch * depth * width,
                bytes_accessed=2 * (2 * span * batch * head_size + depth * width),
                transcendentals=span * batch * per_group,
            ),
        )(lengths, queries, keys, values, out_weight)

    return jax.shard_map(
        body,
        mesh=mesh,
        in_specs=(
            P("groups", None, None),
            P(("tensor", "seq"), "groups", None),
            P(("tensor", "seq"), "groups", None),
            P("groups"),
            P(("tensor", "seq"), None),
        ),
        out_specs=P("groups", ("tensor", "seq")),
        check_vma=False,
    )
```

time: 111 us -> 42.1 us (0.38)
  waiting for transfers between devices: 61 us -> 0 us
  Pallas kernels: 0 us -> 40.5 us
  matrix products: 31.8 us -> 0 us
  between operations: 13.5 us -> 0.01 us
  other arithmetic: 3.33 us -> 0 us
  starting transfers between devices: 1.15 us -> 0 us
  local copies, waits for them, and re-layouts: 0.24 us -> 1.38 us
    reduce_scatter x1 -> x0, waiting for transfers between devices: 60.2 us -> none  [body(): lax.psum_scatter(lax.dot_general(out_weight, attended, (((0,), (1,)), (()...]
    pallas_call x0 -> x1, Pallas kernels: none -> 40.5 us  [body(): pl.pallas_call(functools.partial(kernel, n_tensor, n_seq), out_shape=jax....]
    dot_general x3 -> x0, matrix products: 31.8 us -> none  [the longest x1 15.2 us: body(): jnp.einsum('bgd,pbd->bgp', group_queries, keys, preferred_element_type=jn...]
    convert_element_type x2 -> x0, other arithmetic: 1.63 us -> none  [the longest x1 1.46 us: body(): return mixed_rows.T.astype(jnp.bfloat16)]
    ppermute x3 -> x0, starting transfers between devices: 1.15 us -> none  [swapped(): return lax.ppermute(block, axis, route)]
    unnamed x6 -> x1, local copies, waits for them, and re-layouts: 0.24 us -> 1.38 us
  transfers between devices with their start and end apart: 4 -> 0, of which waited for: 2 -> 0; matrix products, arithmetic and copies ran while one was open for 13% -> 0% of each run, Pallas kernels for 0% -> 0%
where the time goes in v1:
time: 42.1 us; the launch traced here: 41.9 us
  Pallas kernels  40.5 us (96%)
  local copies, waits for them, and re-layouts  1.38 us (3%)
    pallas_call x1, Pallas kernels, body(): pl.pallas_call(functools.partial(kernel, n_tensor, n_seq), out_shape=jax....  40.5 us
    unnamed x1, local copies, waits for them, and re-layouts  1.38 us

profile of v1, /device:TPU:0, one launch (start us, length us, event | category | flops | bytes accessed | tf_op | source)
XLA Modules:
  0.0 41.9 jit_solution(13491906114187352801)
XLA Ops:
  0.0 40.5 %shard_map.55 = bf16[32,512]{1,0:T(8,128)(2,1)} custom-call(s32[32]{0:T(128)} %lengths.1, bf16[32,64,128]{2,1,0:T(8,128)(2,1)} %queries.1, bf16[2048,32,128]{2,1,0:T(8,128)(2,1)} %keys.1, bf16[2048,32,128]{2,1,0:T(8,128)(2,1)} %values.1, bf16[512,8192]{1,0:T(8,128)(2,1)} %weight.1), custom_call_target="tpu_custom_call" | custom-call | flops 536870912 | bytes 41943040 | tf_op jit(solution)/shard_map/pallas_call | solution.py:284
  40.6 1.4 %copy.7 = bf16[32,512]{1,0:T(8,128)(2,1)} copy(bf16[32,512]{1,0:T(8,128)(2,1)} %shard_map.55) | data formatting | bytes 65536

commit v2 on v1

--- a/solution.py
+++ b/solution.py
@@ -15,7 +15,7 @@
 MESH = pl.DeviceIdType.MESH
 masked_fill = -1e30
 ROWS = 16
-STEP = 64
+STEP = 128
 
 
 def kernel(
@@ -168,20 +168,18 @@
                 ).astype(jnp.bfloat16)
             )
         spread = jnp.stack(spread, axis=1).reshape(STEP * ROWS, wide)
-        piece = vbuf[pl.ds(c * STEP, STEP)]
-        for g in range(groups):
-            acc[g] += lax.dot_general(
-                piece[:, g * ROWS:(g + 1) * ROWS].reshape(STEP * ROWS, head_size),
-                spread[:, g * lanes:(g + 1) * lanes],
-                (((0,), (0,)), ((), ())),
-                preferred_element_type=jnp.float32,
-            )
+        acc[...] += lax.dot_general(
+            side_by_side(vbuf, c), spread, (((0,), (0,)), ((), ())),
+            preferred_element_type=jnp.float32,
+        )
         return totals + jnp.sum(share, axis=0)
 
     totals = lax.fori_loop(0, n_chunks, value_step, jnp.zeros((8, wide), jnp.float32))
     totals = jnp.broadcast_to(jnp.sum(totals, axis=0, keepdims=True), (8, wide))
     for g in range(groups):
-        stats[0:head_size, g * lanes:(g + 1) * lanes] = acc[g]
+        stats[0:head_size, g * lanes:(g + 1) * lanes] = acc[
+            g * head_size:(g + 1) * head_size, g * lanes:(g + 1) * lanes
+        ]
     stats[head_size:head_size + 8] = highest
     stats[head_size + 8:head_size + 16] = totals
 
@@ -294,7 +292,7 @@
                 pltpu.VMEM((batch, per_group, head_size), f32),
                 pltpu.VMEM((groups * head_size, wide), bf16),
                 pltpu.VMEM((span // 8, 8, wide), f32),
-                pltpu.VMEM((groups, head_size, lanes), f32),
+                pltpu.VMEM((groups * head_size, wide), f32),
                 pltpu.VMEM((head_size + 16, wide), f32),
                 pltpu.VMEM((peers, head_size + 16, wide), f32),
                 pltpu.VMEM((groups, lanes, head_size), f32),

time: 42.1 us -> 36.1 us (0.86)
  Pallas kernels: 40.5 us -> 34.5 us
    pallas_call x1, Pallas kernels: 40.5 us -> 34.5 us  [body(): pl.pallas_call(functools.partial(kernel, n_tensor, n_seq), out_shape=jax....]
where the time goes in v2:
time: 36.1 us; the launch traced here: 35.9 us
  Pallas kernels  34.5 us (96%)
  local copies, waits for them, and re-layouts  1.38 us (4%)
    pallas_call x1, Pallas kernels, body(): pl.pallas_call(functools.partial(kernel, n_tensor, n_seq), out_shape=jax....  34.5 us
    unnamed x1, local copies, waits for them, and re-layouts  1.38 us

profile of v2, /device:TPU:0, one launch (start us, length us, event | category | flops | bytes accessed | tf_op | source)
XLA Modules:
  0.0 35.9 jit_solution(340799593323583456)
XLA Ops:
  0.0 34.5 %shard_map.55 = bf16[32,512]{1,0:T(8,128)(2,1)} custom-call(s32[32]{0:T(128)} %lengths.1, bf16[32,64,128]{2,1,0:T(8,128)(2,1)} %queries.1, bf16[2048,32,128]{2,1,0:T(8,128)(2,1)} %keys.1, bf16[2048,32,128]{2,1,0:T(8,128)(2,1)} %values.1, bf16[512,8192]{1,0:T(8,128)(2,1)} %weight.1), custom_call_target="tpu_custom_call" | custom-call | flops 536870912 | bytes 41943040 | tf_op jit(solution)/shard_map/pallas_call | solution.py:282
  34.5 1.4 %copy.7 = bf16[32,512]{1,0:T(8,128)(2,1)} copy(bf16[32,512]{1,0:T(8,128)(2,1)} %shard_map.55) | data formatting | bytes 65536

commit v3 on v2

v3 whole, which is shorter than its diff:
```python
import functools
import math

import jax
import jax.numpy as jnp
from jax import lax
from jax.experimental import pallas as pl
from jax.experimental.pallas import tpu as pltpu
from jax.sharding import PartitionSpec as P

HQ = 64
KVH = 8
CACHE = 4096

MESH = pl.DeviceIdType.MESH
masked_fill = -1e30
ROWS = 16
STEP = 128
SIDES = 2


def kernel(
    n_tensor, n_seq, lengths, queries, keys, values, weight, out,
    kbuf, vbuf, wbuf, qbuf, qflat, qdiag, scores, acc, stats, got, flat_att,
    part, from_core, pair, from_near, line, from_far,
    k_sem, v_sem, w_sem, q_sem, stat_sems, core_sems, near_sems, far_sems,
):
    n_flat = n_tensor * n_seq
    span, batch, head_size = keys.shape
    per_group = HQ // KVH
    n_split = CACHE // span
    groups = batch // ROWS
    lanes = ROWS * per_group
    wide = SIDES * lanes
    reach = span // SIDES
    heads_own = HQ // n_flat
    n_chunks = reach // STEP
    cols = out.shape[1]
    n_far = n_tensor // 2
    wide_cols = 2 * n_seq * cols
    scale = 1.0 / math.sqrt(head_size)

    group = lax.axis_index("groups")
    tensor = lax.axis_index("tensor")
    core = lax.axis_index("seq")
    flat = tensor * n_seq + core
    kv_head = flat // n_split
    place = flat % n_split
    far, near = tensor // 2, tensor % 2
    other_core = 1 - core

    offsets = sorted(range(n_far), key=lambda off: (-min(off, n_far - off), off))

    def member(index):
        return (group, index // n_seq, index % n_seq)

    stat_peers = [member(kv_head * n_split + (place + k) % n_split) for k in range(1, n_split)]
    core_peer = (group, tensor, other_core)
    near_peer = (group, far * 2 + 1 - near, core)
    far_peers = [(group, (far + off) % n_far * 2 + near, core) for off in offsets]

    barrier = pltpu.get_barrier_semaphore()
    greeted = stat_peers + [core_peer, near_peer] + [
        peer for off, peer in zip(offsets, far_peers) if off
    ]
    for peer in greeted:
        pl.semaphore_signal(barrier, inc=1, device_id=peer, device_id_type=MESH)

    q_rows = ROWS if per_group < ROWS else per_group
    q_start = pl.multiple_of(kv_head * per_group // q_rows * q_rows, q_rows)
    q_copy = pltpu.make_async_copy(queries.at[:, pl.ds(q_start, q_rows), :], qbuf, q_sem)
    q_copy.start()

    def cache_copy(cache, buf, sems, g, side, c):
        piece = pl.ds(side * reach + c * STEP, STEP)
        return pltpu.make_async_copy(
            cache.at[piece, g * ROWS:(g + 1) * ROWS], buf.at[g, piece], sems.at[g, side, c]
        )

    def start_cache(cache, buf, sems, g):
        @pl.loop(0, n_chunks)
        def _(c):
            for side in range(SIDES):
                cache_copy(cache, buf, sems, g, side, c).start()

    def w_copy(k):
        start = pl.multiple_of((far + offsets[k]) % n_far * wide_cols, wide_cols)
        return pltpu.make_async_copy(weight.at[:, pl.ds(start, wide_cols)], wbuf.at[k], w_sem.at[k])

    for g in range(groups):
        start_cache(keys, kbuf, k_sem, g)
        if g == groups - 1:
            for k in range(n_far):
                w_copy(k).start()
        start_cache(values, vbuf, v_sem, g)

    lane = lax.broadcasted_iota(jnp.int32, (8, wide), 1)
    sub = lax.broadcasted_iota(jnp.int32, (8, wide), 0)
    home = lane % 8
    low = lane % ROWS < 8
    turn = (sub - home + 8) % 8
    at_home = sub == home
    keep_low = at_home & low
    keep_high = at_home & jnp.logical_not(low)
    taken = place * span + lane // lanes * reach + turn

    def room_of(g):
        live_slots = jnp.zeros((8, wide), jnp.int32)
        for b in range(ROWS):
            live_slots = jnp.where(lane % ROWS == b, lengths[g * ROWS + b], live_slots)
        return live_slots - taken

    q_copy.wait()
    q = qbuf[...].astype(jnp.float32)
    if q_rows > per_group:
        q = jnp.where(kv_head % 2 == 0, q[:, :per_group], q[:, per_group:])
    qflat[...] = q
    qdiag[...] = jnp.zeros_like(qdiag)
    for g in range(groups):
        block = jnp.concatenate(
            [qflat[g * ROWS:(g + 1) * ROWS, j, :] for j in range(per_group)], axis=0
        ).T.astype(jnp.bfloat16)
        for side in range(SIDES):
            qdiag[
                g, side * head_size:(side + 1) * head_size, side * lanes:(side + 1) * lanes
            ] = block

    def side_by_side(buf, g, c):
        return jnp.concatenate(
            [
                buf[g, pl.ds(side * reach + c * STEP, STEP)].reshape(STEP * ROWS, head_size)
                for side in range(SIDES)
            ],
            axis=1,
        )

    blocks = STEP // 8

    def base_of(c):
        return c * STEP + 8 * lax.broadcasted_iota(jnp.int32, (blocks, 8, wide), 0)

    def both_sides(row, merge):
        return functools.reduce(
            merge, [row[:, side * lanes:(side + 1) * lanes] for side in range(SIDES)]
        )

    def score_pass(g, room):
        def step(c, highest):
            for side in range(SIDES):
                cache_copy(keys, kbuf, k_sem, g, side, c).wait()
            product = jnp.dot(
                side_by_side(kbuf, g, c), qdiag[g], preferred_element_type=jnp.float32
            ).reshape(blocks, 8, 2, 8, wide)
            merged = jnp.where(low, product[:, :, 0], product[:, :, 1])
            dense = merged[:, 0]
            for i in range(1, 8):
                dense = jnp.where(turn == i, pltpu.roll(merged[:, i], i, 1), dense)
            dense = jnp.where(base_of(c) < room, dense, masked_fill)
            scores[pl.ds(c * blocks, blocks)] = dense
            return jnp.maximum(highest, jnp.max(dense, axis=0))

        highest = lax.fori_loop(0, n_chunks, step, jnp.full((8, wide), masked_fill, jnp.float32))
        return both_sides(jnp.max(highest, axis=0, keepdims=True), jnp.maximum)

    def value_pass(g, room, highest, first, last, totals):
        level = jnp.broadcast_to(jnp.concatenate([highest] * SIDES, axis=1), (8, wide))

        def step(c, totals):
            for side in range(SIDES):
                cache_copy(values, vbuf, v_sem, g, side, c).wait()
            dense = scores[pl.ds(c * blocks, blocks)]
            share = jnp.where(base_of(c) < room, jnp.exp((dense - level) * scale), 0.0)
            spread = []
            for i in range(8):
                turned = pltpu.roll(share, 8 - i, 1) if i else share
                spread.append(
                    jnp.concatenate(
                        [jnp.where(keep_low, turned, 0.0), jnp.where(keep_high, turned, 0.0)],
                        axis=1,
                    ).astype(jnp.bfloat16)
                )
            spread = jnp.stack(spread, axis=1).reshape(STEP * ROWS, wide)
            acc[...] += lax.dot_general(
                side_by_side(vbuf, g, c), spread, (((0,), (0,)), ((), ())),
                preferred_element_type=jnp.float32,
            )
            return totals + jnp.sum(share, axis=0)

        return lax.fori_loop(first, last, step, totals)

    sends = []

    def send(source, target, sems, slot, peer):
        copy = pltpu.make_async_remote_copy(
            src_ref=source, dst_ref=target,
            send_sem=sems.at[(0,) + slot], recv_sem=sems.at[(1,) + slot],
            device_id=peer, device_id_type=MESH,
        )
        copy.start()
        sends.append(copy)
        return copy

    def send_stats(g, highest, totals):
        stats[g, 0:head_size] = functools.reduce(
            jnp.add,
            [
                acc[side * head_size:(side + 1) * head_size, side * lanes:(side + 1) * lanes]
                for side in range(SIDES)
            ],
        )
        total = both_sides(jnp.sum(totals, axis=0, keepdims=True), jnp.add)
        stats[g, head_size:head_size + 8] = jnp.broadcast_to(highest, (8, lanes))
        stats[g, head_size + 8:head_size + 16] = jnp.broadcast_to(total, (8, lanes))
        return [
            send(stats.at[g], got.at[g, i], stat_sems, (g, i), peer)
            for i, peer in enumerate(stat_peers)
        ]

    def attended_of(g, copies):
        for copy in copies:
            copy.wait_recv()
        sources = [stats.at[g]] + [got.at[g, i] for i in range(n_split - 1)]
        tops = [source[head_size:head_size + 1] for source in sources]
        top = functools.reduce(jnp.maximum, tops)
        total = jnp.zeros((1, lanes), jnp.float32)
        summed = jnp.zeros((head_size, lanes), jnp.float32)
        for source, own_top in zip(sources, tops):
            factor = jnp.exp((own_top - top) * scale)
            total = total + source[head_size + 8:head_size + 9] * factor
            summed = summed + source[0:head_size] * factor
        flat_att[g] = (summed / total).T
        start = pl.multiple_of(place * heads_own * ROWS, ROWS)
        return jnp.concatenate(
            [flat_att[g, pl.ds(start + j * ROWS, ROWS), :] for j in range(heads_own)], axis=1
        ).astype(jnp.bfloat16)

    core_copies, near_copies, far_copies = {}, {}, {}

    def project(g, attended, k):
        if g == 0:
            w_copy(k).wait()
        for n in range(2):
            for s in range(n_seq):
                at = (n * n_seq + s) * cols
                part[g, k, s, n] = jnp.dot(
                    attended, wbuf[k, :, at:at + cols], preferred_element_type=jnp.float32
                )
        core_copies[g, k] = send(
            part.at[g, k, other_core], from_core.at[g, k], core_sems, (g, k), core_peer
        )

    def to_near(g, k):
        core_copies[g, k].wait_recv()
        pair[g, k] = part[g, k, core] + from_core[g, k]
        near_copies[g, k] = send(
            pair.at[g, k, 1 - near], from_near.at[g, k], near_sems, (g, k), near_peer
        )

    def to_far(g, k):
        near_copies[g, k].wait_recv()
        line[g, k] = pair[g, k, near] + from_near[g, k]
        if offsets[k]:
            far_copies[g, k] = send(
                line.at[g, k], from_far.at[g, k], far_sems, (g, k), far_peers[k]
            )

    waiting = None
    for g in range(groups):
        room = room_of(g)
        highest = score_pass(g, room)
        if g:
            attended = attended_of(g - 1, waiting)
            for k in range(n_far):
                project(g - 1, attended, k)
        acc[...] = jnp.zeros_like(acc)
        totals = jnp.zeros((8, wide), jnp.float32)
        if g:
            cuts = [0, n_chunks // 4, n_chunks * 3 // 4, n_chunks]
            totals = value_pass(g, room, highest, cuts[0], cuts[1], totals)
            for k in range(n_far):
                to_near(g - 1, k)
            totals = value_pass(g, room, highest, cuts[1], cuts[2], totals)
            for k in range(n_far):
                to_far(g - 1, k)
            totals = value_pass(g, room, highest, cuts[2], cuts[3], totals)
        else:
            totals = value_pass(g, room, highest, 0, n_chunks, totals)
            pl.semaphore_wait(barrier, len(greeted))
        waiting = send_stats(g, highest, totals)

    g = groups - 1
    attended = attended_of(g, waiting)
    for step in range(n_far + 2):
        if step < n_far:
            project(g, attended, step)
        if 0 <= step - 1 < n_far:
            to_near(g, step - 1)
        if 0 <= step - 2 < n_far:
            to_far(g, step - 2)
    for g in range(groups):
        result = line[g, n_far - 1]
        for k in range(n_far - 1):
            far_copies[g, k].wait_recv()
            result = result + from_far[g, k]
        out[g * ROWS:(g + 1) * ROWS] = result.astype(out.dtype)
    for copy in sends:
        copy.wait_send()


def solution(mesh):
    n_tensor, n_seq = mesh.shape["tensor"], mesh.shape["seq"]

    def body(queries, keys, values, lengths, out_weight):
        span, batch, head_size = keys.shape
        depth, width = out_weight.shape
        per_group = HQ // KVH
        n_flat = n_tensor * n_seq
        cols = width // n_flat
        n_far = n_tensor // 2
        n_split = CACHE // span
        groups = batch // ROWS
        lanes = ROWS * per_group
        wide = SIDES * lanes
        n_chunks = span // SIDES // STEP
        q_rows = max(ROWS, per_group)
        f32, bf16 = jnp.float32, jnp.bfloat16
        peers = max(1, n_split - 1)
        return pl.pallas_call(
            functools.partial(kernel, n_tensor, n_seq),
            out_shape=jax.ShapeDtypeStruct((batch, cols), bf16),
            in_specs=[pl.BlockSpec(memory_space=pltpu.SMEM)] + [pl.BlockSpec(memory_space=pl.ANY)] * 4,
            out_specs=pl.BlockSpec(memory_space=pltpu.VMEM),
            scratch_shapes=[
                pltpu.VMEM((groups, span, ROWS, head_size), bf16),
                pltpu.VMEM((groups, span, ROWS, head_size), bf16),
                pltpu.VMEM((n_far, depth, 2 * n_seq * cols), bf16),
                pltpu.VMEM((batch, q_rows, head_size), bf16),
                pltpu.VMEM((batch, per_group, head_size), f32),
                pltpu.VMEM((groups, SIDES * head_size, wide), bf16),
                pltpu.VMEM((span // SIDES // 8, 8, wide), f32),
                pltpu.VMEM((SIDES * head_size, wide), f32),
                pltpu.VMEM((groups, head_size + 16, lanes), f32),
                pltpu.VMEM((groups, peers, head_size + 16, lanes), f32),
                pltpu.VMEM((groups, lanes, head_size), f32),
                pltpu.VMEM((groups, n_far, n_seq, 2, ROWS, cols), f32),
                pltpu.VMEM((groups, n_far, 2, ROWS, cols), f32),
                pltpu.VMEM((groups, n_far, 2, ROWS, cols), f32),
                pltpu.VMEM((groups, n_far, ROWS, cols), f32),
                pltpu.VMEM((groups, n_far, ROWS, cols), f32),
                pltpu.VMEM((groups, n_far, ROWS, cols), f32),
                pltpu.SemaphoreType.DMA((groups, SIDES, n_chunks)),
                pltpu.SemaphoreType.DMA((groups, SIDES, n_chunks)),
                pltpu.SemaphoreType.DMA((n_far,)),
                pltpu.SemaphoreType.DMA,
                pltpu.SemaphoreType.DMA((2, groups, peers)),
                pltpu.SemaphoreType.DMA((2, groups, n_far)),
                pltpu.SemaphoreType.DMA((2, groups, n_far)),
                pltpu.SemaphoreType.DMA((2, groups, n_far)),
            ],
            compiler_params=pltpu.CompilerParams(
                collective_id=0, has_side_effects=True, vmem_limit_bytes=60 * 1024 * 1024
            ),
            cost_estimate=pl.CostEstimate(
                flops=4 * span * batch * head_size * per_group + 2 * batch * depth * width,
                bytes_accessed=2 * (2 * span * batch * head_size + depth * width),
                transcendentals=span * batch * per_group,
            ),
        )(lengths, queries, keys, values, out_weight)

    return jax.shard_map(
        body,
        mesh=mesh,
        in_specs=(
            P("groups", None, None),
            P(("tensor", "seq"), "groups", None),
            P(("tensor", "seq"), "groups", None),
            P("groups"),
            P(("tensor", "seq"), None),
        ),
        out_specs=P("groups", ("tensor", "seq")),
        check_vma=False,
    )
```

time: 36.1 us -> 38.6 us (1.069)
  Pallas kernels: 34.5 us -> 37 us
    pallas_call x1, Pallas kernels: 34.5 us -> 37 us  [body(): pl.pallas_call(functools.partial(kernel, n_tensor, n_seq), out_shape=jax....]
where the time goes in v3:
time: 38.6 us; the launch traced here: 38.4 us
  Pallas kernels  37 us (96%)
  local copies, waits for them, and re-layouts  1.38 us (4%)
    pallas_call x1, Pallas kernels, body(): pl.pallas_call(functools.partial(kernel, n_tensor, n_seq), out_shape=jax....  37 us
    unnamed x1, local copies, waits for them, and re-layouts  1.38 us

profile of v3, /device:TPU:0, one launch (start us, length us, event | category | flops | bytes accessed | tf_op | source)
XLA Modules:
  0.0 38.4 jit_solution(16858067402421880360)
XLA Ops:
  0.0 37.0 %shard_map.55 = bf16[32,512]{1,0:T(8,128)(2,1)} custom-call(s32[32]{0:T(128)} %lengths.1, bf16[32,64,128]{2,1,0:T(8,128)(2,1)} %queries.1, bf16[2048,32,128]{2,1,0:T(8,128)(2,1)} %keys.1, bf16[2048,32,128]{2,1,0:T(8,128)(2,1)} %values.1, bf16[512,8192]{1,0:T(8,128)(2,1)} %weight.1), custom_call_target="tpu_custom_call" | custom-call | flops 536870912 | bytes 41943040 | tf_op jit(solution)/shard_map/pallas_call | solution.py:328
  37.0 1.4 %copy.7 = bf16[32,512]{1,0:T(8,128)(2,1)} copy(bf16[32,512]{1,0:T(8,128)(2,1)} %shard_map.55) | data formatting | bytes 65536

commit v4 on v2

--- a/solution.py
+++ b/solution.py
@@ -15,7 +15,7 @@
 MESH = pl.DeviceIdType.MESH
 masked_fill = -1e30
 ROWS = 16
-STEP = 128
+STEP = 256
 
 
 def kernel(
@@ -152,8 +152,13 @@
     scale = 1.0 / math.sqrt(head_size)
 
     acc[...] = jnp.zeros_like(acc)
-    keep_low = at_home & low
-    keep_high = at_home & jnp.logical_not(low)
+    keep = jnp.concatenate(
+        [
+            jnp.where(at_home & low, 1.0, 0.0),
+            jnp.where(at_home & jnp.logical_not(low), 1.0, 0.0),
+        ],
+        axis=0,
+    ).astype(jnp.bfloat16)
 
     def value_step(c, totals):
         v_copy(c).wait()
@@ -163,9 +168,7 @@
         for i in range(8):
             turned = pltpu.roll(share, 8 - i, 1) if i else share
             spread.append(
-                jnp.concatenate(
-                    [jnp.where(keep_low, turned, 0.0), jnp.where(keep_high, turned, 0.0)], axis=1
-                ).astype(jnp.bfloat16)
+                jnp.concatenate([turned, turned], axis=1).astype(jnp.bfloat16) * keep
             )
         spread = jnp.stack(spread, axis=1).reshape(STEP * ROWS, wide)
         acc[...] += lax.dot_general(

time: 36.1 us -> 33.2 us (0.920)
  Pallas kernels: 34.5 us -> 31.6 us
    pallas_call x1, Pallas kernels: 34.5 us -> 31.6 us  [body(): pl.pallas_call(functools.partial(kernel, n_tensor, n_seq), out_shape=jax....]
where the time goes in v4:
time: 33.2 us; the launch traced here: 33 us
  Pallas kernels  31.6 us (95%)
  local copies, waits for them, and re-layouts  1.38 us (4%)
    pallas_call x1, Pallas kernels, body(): pl.pallas_call(functools.partial(kernel, n_tensor, n_seq), out_shape=jax....  31.6 us
    unnamed x1, local copies, waits for them, and re-layouts  1.38 us

profile of v4, /device:TPU:0, one launch (start us, length us, event | category | flops | bytes accessed | tf_op | source)
XLA Modules:
  0.0 33.0 jit_solution(8392421162045029511)
XLA Ops:
  0.0 31.6 %shard_map.55 = bf16[32,512]{1,0:T(8,128)(2,1)} custom-call(s32[32]{0:T(128)} %lengths.1, bf16[32,64,128]{2,1,0:T(8,128)(2,1)} %queries.1, bf16[2048,32,128]{2,1,0:T(8,128)(2,1)} %keys.1, bf16[2048,32,128]{2,1,0:T(8,128)(2,1)} %values.1, bf16[512,8192]{1,0:T(8,128)(2,1)} %weight.1), custom_call_target="tpu_custom_call" | custom-call | flops 536870912 | bytes 41943040 | tf_op jit(solution)/shard_map/pallas_call | solution.py:285
  31.6 1.4 %copy.7 = bf16[32,512]{1,0:T(8,128)(2,1)} copy(bf16[32,512]{1,0:T(8,128)(2,1)} %shard_map.55) | data formatting | bytes 65536
